TPU v7x, 256 devices: a whole 4x4x8 slice. The times are simulated.
256 devices in a mesh: layer: 4 (over z_lo, core), latent: 64 (over x, z_hi, y).
Axes of the slice: x: 4, y: 4, z: 8 (z_hi: 4, z_lo: 2; z = z_hi * 2 + z_lo), core: 2. Of those that a mesh axis runs over, the one named last changes fastest.
Arguments:
- acts: bfloat16 [4, 512, 2048], P('layer', None, 'latent'), may hold values from -6 to 6
- w_enc: bfloat16 [4, 2048, 32768], P('layer', None, 'latent'), may hold values from -0.0625 to 0.0625
- b_enc: float32 [32768], P('latent'), may hold values from -3 to 3
- w_dec: bfloat16 [4, 32768, 2048], P('layer', 'latent'), may hold values from -0.09375 to 0.09375
- b_dec: bfloat16 [4, 2048], P('layer', 'latent'), may hold values from -3 to 3
Outputs:
- grad_enc: bfloat16 [4, 2048, 32768], P('layer', None, 'latent')
- grad_dec: bfloat16 [4, 32768, 2048], P('layer', 'latent')
- grad_benc: float32 [32768], P('latent')
- grad_bdec: float32 [4, 2048], P('layer', 'latent')
All inputs are finite; a program needn't handle non-finite values.
Results may differ from a plain program's by a relative error of at most 0.014.
Values may be sent and summed in bfloat16 or wider, within the bound.
No kernel may reach another device: no remote copies, remote signals or barrier semaphores. Data moves between devices by JAX's collectives and lax.ppermute only.
A program may use at most 64 MiB of HBM per device.

v0:
```python
import jax
import jax.numpy as jnp
from jax import lax
from jax.sharding import Mesh
from jax.sharding import PartitionSpec as P

LATENT = ("latent_0", "latent_1", "latent_2")


def turned_gather(arrays, axis, dims):
    turned = [jnp.moveaxis(a, dim, 0) for a, dim in zip(arrays, dims)]
    widths = [t[0].size for t in turned]
    both = jnp.concatenate([t.reshape(-1, w) for t, w in zip(turned, widths)], axis=1)
    whole = lax.all_gather(both, axis, axis=0, tiled=True)
    blocks = jnp.split(whole, [sum(widths[:k]) for k in range(1, len(widths))], axis=1)
    return tuple(
        (
            jnp.moveaxis(b.reshape(-1, *t.shape[1:]), 0, dim)
            for b, t, dim in zip(blocks, turned, dims)
        )
    )


def sent_to_all(x, axis):
    peers = lax.axis_size(axis)
    return lax.all_to_all(jnp.broadcast_to(x[None], (peers, *x.shape)), axis, 0, 0, tiled=True)


def over_copies(x, axis):
    everything = sent_to_all(x, axis)
    return jnp.sum(everything, axis=0)


def sum_in_order(blocks, axes, order):
    inside = blocks.shape[1:]
    blocks = blocks.reshape(*(lax.axis_size(a) for a in axes), *inside)
    blocks = jnp.moveaxis(blocks, order, range(len(axes))).reshape(-1, *inside)
    for k in order:
        blocks = lax.psum_scatter(blocks, axes[k], scatter_dimension=0, tiled=True)
    return blocks[0]


def in_blocks(x, dim, peers):
    before, after = (x.shape[:dim], x.shape[dim + 1 :])
    return jnp.moveaxis(x.reshape(*before, peers, -1, *after), dim, 0)


def summed_rows(x, axes, order, dim):
    peers = lax.axis_size(axes)
    return sum_in_order(in_blocks(x, dim, peers), axes, order)


def taken_together(x, axis):
    everything = sent_to_all(x, axis)
    return jnp.sum(everything.astype(jnp.float32), axis=0)


def body(acts, w_enc, b_enc, w_dec, b_dec):
    local = acts[0]
    width_own = local.shape[1]
    enc_own = w_enc[0]
    dec_own = w_dec[0]
    full, bias_full = turned_gather((local, b_dec), LATENT, (1, 1))
    tokens_all = full.shape[0]
    scale = tokens_all ** (-0.5)
    part = jnp.dot(full, enc_own, preferred_element_type=jnp.float32)
    pre = over_copies(part, "layer") + b_enc[None, :]
    feat = (jax.nn.softplus(4.0 * pre) / 4.0).astype(jnp.bfloat16)
    rows = tokens_all // lax.axis_size(LATENT)
    recon = summed_rows(
        jnp.dot(feat, dec_own, preferred_element_type=jnp.float32), LATENT, (0, 2, 1), 0
    )
    position = lax.axis_index(LATENT)
    own_rows = lax.dynamic_slice_in_dim(full, position * rows, rows, 0)
    err_rows = (recon + bias_full.astype(jnp.float32) - own_rows.astype(jnp.float32)).astype(
        jnp.bfloat16
    )
    err = lax.all_gather(err_rows, LATENT, axis=0, tiled=True)
    bias_grad_full = scale * jnp.sum(err.astype(jnp.float32), axis=0)
    grad_bdec = lax.dynamic_slice_in_dim(bias_grad_full, position * width_own, width_own, 0)
    dec_prod = lax.dot_general(
        feat, err, (((0,), (0,)), ((), ())), preferred_element_type=jnp.float32
    )
    grad_dec = (scale * dec_prod).astype(jnp.bfloat16)
    feat_term = lax.dot_general(
        err, dec_own, (((1,), (1,)), ((), ())), preferred_element_type=jnp.float32
    )
    grad_feat = scale * taken_together(feat_term.astype(jnp.bfloat16), "layer").astype(jnp.float32)
    grad_pre = grad_feat * jax.nn.sigmoid(4.0 * pre)
    grad_benc = jnp.sum(grad_pre, axis=0)
    grad_pre_b = grad_pre.astype(jnp.bfloat16)
    enc_prod = lax.dot_general(
        full, grad_pre_b, (((0,), (0,)), ((), ())), preferred_element_type=jnp.float32
    )
    grad_enc = enc_prod.astype(jnp.bfloat16)
    return (grad_enc[None], grad_dec[None], grad_benc, grad_bdec[None])


def solution(mesh):
    finer = Mesh(
        mesh.devices.reshape(mesh.shape["layer"], 4, 4, 4),
        ("layer", "latent_0", "latent_1", "latent_2"),
    )
    placed = (
        P("layer", None, LATENT),
        P("layer", None, LATENT),
        P(LATENT),
        P("layer", LATENT, None),
        P("layer", LATENT),
    )
    return jax.shard_map(
        body,
        mesh=finer,
        in_specs=placed,
        out_specs=(
            P("layer", None, LATENT),
            P("layer", LATENT, None),
            P(LATENT),
            P("layer", LATENT),
        ),
        check_vma=False,
    )
```

profile of v0, /device:TPU:1, one launch (start us, length us, event | category | flops | bytes accessed | tf_op | source)
XLA Modules:
  0.0 392.8 jit_solution(11635537470442020400)
XLA Ops:
  7.2 0.9 copy.15
  8.1 1.4 pad_maximum_fusion
  9.5 0.0 reduce-scatter.4.cloned.1.call-start
  9.6 86.1 %all-gather.3.cloned.1.call-done = bf16[2048,513]{1,0:T(8,128)(2,1)} async-done(((bf16[32,513]{1,0:T(8,128)(2,1)}), bf16[2048,513]{1,0:T(8,128)(2,1)}) %all-gather.3.cloned.1.call-update) | async-done | bytes 2101264 | tf_op jit(solution)/shard_map/all_gather | solution.py:14
  95.7 3.5 fusion.5
  99.2 0.5 broadcast_in_dim.10
  99.7 52.5 %all_to_all.10 = f32[4,512,512]{2,1,0:T(8,128)} all-to-all(f32[4,512,512]{2,1,0:T(8,128)S(1)} %broadcast_in_dim.10), channel_id=1, replica_groups=mesh['layer'=4,'latent_0'=4,'latent_1'=4,'latent_2'=4] {'layer'}, dimensions={0} | all-to-all | bytes 8388608 | tf_op jit(solution)/shard_map/all_to_all | solution.py:26
  152.2 2.8 reduce_sum.36
  155.0 0.7 fusion.11
  155.8 0.8 copy-done.3
  156.6 1.2 convolution_bitcast_fusion
  157.8 2.2 copy.17
  160.1 47.6 %reduce-scatter.4.cloned.1.call-done = f32[16,8,2048]{2,1,0:T(8,128)} async-done(((f32[64,8,2048]{2,1,0:T(8,128)}), f32[16,8,2048]{2,1,0:T(8,128)}) %reduce-scatter.4.cloned.1.call-update) | async-done | bytes 1048592 | tf_op jit(solution)/shard_map/reduce_scatter | solution.py:39
  207.7 26.4 %reduce-scatter.6.cloned.1.call-done = f32[4,8,2048]{2,1,0:T(8,128)} async-done(((f32[16,8,2048]{2,1,0:T(8,128)}), f32[4,8,2048]{2,1,0:T(8,128)}) %reduce-scatter.6.cloned.1.call-update) | async-done | bytes 262160 | tf_op jit(solution)/shard_map/reduce_scatter | solution.py:39
  234.2 1.6 slice-done
  235.8 1.0 constant_dynamic-slice_fusion
  236.8 1.2 copy.20
  238.0 1.3 convert_reduce_fusion.2
  239.3 22.5 %reduce-scatter.8.cloned.1.call-done = f32[1,8,2048]{2,1,0:T(8,128)} async-done(((f32[4,8,2048]{2,1,0:T(8,128)}), f32[1,8,2048]{2,1,0:T(8,128)}) %reduce-scatter.8.cloned.1.call-update) | async-done | bytes 65552 | tf_op jit(solution)/shard_map/reduce_scatter | solution.py:39
  261.8 1.5 fusion.13
  263.3 80.6 %all-gather.5.cloned.1.call-done = bf16[512,2048]{1,0:T(8,128)(2,1)} async-done(((bf16[8,2048]{1,0:T(8,128)(2,1)}), bf16[512,2048]{1,0:T(8,128)(2,1)}) %all-gather.5.cloned.1.call-update) | async-done | bytes 2097168 | tf_op jit(solution)/shard_map/all_gather | solution.py:78
  343.9 2.9 fusion.7
  346.8 1.5 broadcast_in_dim.11
  348.3 6.7 %all-to-all-start.1 = ((bf16[4,512,512]{2,1,0:T(8,128)(2,1)}), bf16[4,512,512]{2,1,0:T(8,128)(2,1)}, u32[]{:S(2)}, u32[]{:S(2)}) async-start(bf16[4,512,512]{2,1,0:T(8,128)(2,1)} %broadcast_in_dim.11), calls=%async_computation.4 | async-start | bytes 4194304 | tf_op jit(solution)/shard_map/all_to_all | solution.py:26
  355.0 2.1 convert_reduce_fusion
  357.1 0.6 fusion.14
  357.7 3.7 fusion.1
  361.3 18.6 %all-to-all-done.1 = bf16[4,512,512]{2,1,0:T(8,128)(2,1)} async-done(((bf16[4,512,512]{2,1,0:T(8,128)(2,1)}), bf16[4,512,512]{2,1,0:T(8,128)(2,1)}, u32[]{:S(2)}, u32[]{:S(2)}) %all-to-all-start.1) | async-done | bytes 2097184 | tf_op jit(solution)/shard_map/all_to_all | solution.py:26
  379.9 2.0 convert_reduce_fusion.1
  382.0 0.9 fusion.17
  382.9 0.8 copy-done.1
  383.7 2.6 fusion
  (18 shorter events, 0.3 us)
Async XLA Ops:
  7.2 149.4 %copy-start = (bf16[1,512,2048]{2,1,0:T(8,128)(2,1)S(1)}, bf16[1,512,2048]{2,1,0:T(8,128)(2,1)}, u32[]{:S(2)}) copy-start(bf16[1,512,2048]{2,1,0:T(8,128)(2,1)} %param.8) | copy-start | bytes 6291460
  7.2 88.5 %all-gather.3.cloned.1.call-start = ((), (), s32[]{:S(2)}) async-start(), calls=%async_computation.5 | async-start | bytes 2662400 | tf_op jit(solution)/shard_map/all_gather | solution.py:14
  9.5 198.1 %reduce-scatter.4.cloned.1.call-start = ((), (), s32[]{:S(2)}) async-start(), calls=%async_computation.6 | async-start | bytes 5242880 | tf_op jit(solution)/shard_map/reduce_scatter | solution.py:39
  152.2 2.8 copy-start.4
  155.8 0.8 copy-start.3
  160.1 74.1 %reduce-scatter.6.cloned.1.call-start = ((), (), s32[]{:S(2)}) async-start(), calls=%async_computation.7 | async-start | bytes 1310720 | tf_op jit(solution)/shard_map/reduce_scatter | solution.py:39
  207.7 54.1 %reduce-scatter.8.cloned.1.call-start = ((), (), s32[]{:S(2)}) async-start(), calls=%async_computation.8 | async-start | bytes 327680 | tf_op jit(solution)/shard_map/reduce_scatter | solution.py:39
  234.2 109.7 %all-gather.5.cloned.1.call-start = ((), (), s32[]{:S(2)}) async-start(), calls=%async_computation.9 | async-start | bytes 2129920 | tf_op jit(solution)/shard_map/all_gather | solution.py:78
  234.2 1.6 slice-start
  348.3 31.7 %all-to-all-start.1 = ((bf16[4,512,512]{2,1,0:T(8,128)(2,1)}), bf16[4,512,512]{2,1,0:T(8,128)(2,1)}, u32[]{:S(2)}, u32[]{:S(2)}) async-start(bf16[4,512,512]{2,1,0:T(8,128)(2,1)} %broadcast_in_dim.11), calls=%async_computation.4 | async-start | bytes 4194304 | tf_op jit(solution)/shard_map/all_to_all | solution.py:26
  355.0 2.7 copy-start.2
  381.9 1.7 copy-start.1
Sparse Core Ops, SparseCore 0:
  11.9 83.7 all-gather.2
  160.2 47.4 reduce-scatter.3
  210.4 23.7 reduce-scatter.5
  236.5 25.2 reduce-scatter.7
  266.0 77.8 all-gather.4
where the time goes:
time: 393 us
  waiting for transfers between devices  282 us (72%)
  blocking collectives  52.5 us (13%)
  between operations  13.9 us (4%)
  matrix products  13.8 us (4%)
  other arithmetic  13.2 us (3%)
  local copies, waits for them, and re-layouts  10.5 us (3%)
  starting transfers between devices  6.93 us (2%)
    reduce_scatter x3, waiting for transfers between devices, sum_in_order(): blocks = lax.psum_scatter(blocks, axes[k], scatter_dimension=0, tiled=True)  96.4 us
    all_gather x1, waiting for transfers between devices, turned_gather(): whole = lax.all_gather(both, axis, axis=0, tiled=True)  86.1 us
    all_gather x1, waiting for transfers between devices, body(): err = lax.all_gather(err_rows, LATENT, axis=0, tiled=True)  80.6 us
    all_to_all x1, blocking collectives, sent_to_all(): lax.all_to_all(jnp.broadcast_to(x[None], (peers, *x.shape)), axis, 0, 0,...  52.5 us
    all_to_all x1, waiting for transfers between devices, sent_to_all(): lax.all_to_all(jnp.broadcast_to(x[None], (peers, *x.shape)), axis, 0, 0,...  18.6 us
  transfers between devices with their start and end apart: 6, of which 6 were waited for; matrix products, arithmetic and copies ran while one was open for 2% of the time, Pallas kernels for 0%

commit v1 on v0

--- a/solution.py
+++ b/solution.py
@@ -11,7 +11,14 @@
     turned = [jnp.moveaxis(a, dim, 0) for a, dim in zip(arrays, dims)]
     widths = [t[0].size for t in turned]
     both = jnp.concatenate([t.reshape(-1, w) for t, w in zip(turned, widths)], axis=1)
-    whole = lax.all_gather(both, axis, axis=0, tiled=True)
+
+    def _unite_pipes(x_local):
+        m_next = jnp.concatenate(
+            lax.all_to_all(jnp.stack(lax.axis_size(axis) * [x_local]), axis, 0, 0), axis=0
+        )
+        return m_next
+
+    whole = _unite_pipes(both)
     blocks = jnp.split(whole, [sum(widths[:k]) for k in range(1, len(widths))], axis=1)
     return tuple(
         (

time: 393 us -> 572 us (1.46)
  waiting for transfers between devices: 282 us -> 371 us
  blocking collectives: 52.5 us -> 131 us
  local copies, waits for them, and re-layouts: 10.5 us -> 23.1 us
    reduce_scatter x3, waiting for transfers between devices: 96.4 us -> 277 us  [sum_in_order(): blocks = lax.psum_scatter(blocks, axes[k], scatter_dimension=0, tiled=True)]
    all_gather x1 -> x0, waiting for transfers between devices: 86.1 us -> none  [turned_gather(): whole = lax.all_gather(both, axis, axis=0, tiled=True)]
    all_to_all x0 -> x1, blocking collectives: none -> 76.2 us  [_unite_pipes(): lax.all_to_all(jnp.stack(lax.axis_size(axis) * [x_local]), axis, 0, 0)]
    reduce_scatter x0 -> x1, local copies, waits for them, and re-layouts: none -> 9.8 us  [sum_in_order(): blocks = lax.psum_scatter(blocks, axes[k], scatter_dimension=0, tiled=True)]
  transfers between devices with their start and end apart: 6 -> 5, of which waited for: 6 -> 5; matrix products, arithmetic and copies ran while one was open for 2% -> 2% of each run, Pallas kernels for 0% -> 0%
where the time goes in v1:
time: 572 us; the launch traced here: 571 us
  waiting for transfers between devices  371 us (65%)
  blocking collectives  131 us (23%)
  local copies, waits for them, and re-layouts  23.1 us (4%)
  between operations  13.9 us (2%)
  other arithmetic  13.8 us (2%)
  matrix products  11.6 us (2%)
  starting transfers between devices  6.91 us (1%)
    reduce_scatter x3, waiting for transfers between devices, sum_in_order(): blocks = lax.psum_scatter(blocks, axes[k], scatter_dimension=0, tiled=True)  277 us
    all_to_all x1, blocking collectives, _unite_pipes(): lax.all_to_all(jnp.stack(lax.axis_size(axis) * [x_local]), axis, 0, 0)  76.2 us
    all_gather x1, waiting for transfers between devices, body(): err = lax.all_gather(err_rows, LATENT, axis=0, tiled=True)  75.3 us
    all_to_all x1, blocking collectives, sent_to_all(): lax.all_to_all(jnp.broadcast_to(x[None], (peers, *x.shape)), axis, 0, 0,...  54.8 us
    all_to_all x1, waiting for transfers between devices, sent_to_all(): lax.all_to_all(jnp.broadcast_to(x[None], (peers, *x.shape)), axis, 0, 0,...  18.6 us
  transfers between devices with their start and end apart: 5, of which 5 were waited for; matrix products, arithmetic and copies ran while one was open for 2% of the time, Pallas kernels for 0%

profile of v1, /device:TPU:1, one launch (start us, length us, event | category | flops | bytes accessed | tf_op | source)
XLA Modules:
  0.0 571.5 jit_solution(752935282036041531)
XLA Ops:
  7.2 0.9 copy.20
  8.1 0.8 pad_maximum_fusion
  9.1 76.2 %all_to_all.15 = bf16[64,32,513]{2,1,0:T(8,128)(2,1)S(1)} all-to-all(bf16[64,32,513]{2,1,0:T(8,128)(2,1)S(1)} %stack.2), channel_id=1, replica_groups=mesh['layer'=4,'latent_0'=4,'latent_1'=4,'latent_2'=4] {'latent_0','late..., dimensions={0} | all-to-all | bytes 4202496 | tf_op jit(solution)/shard_map/all_to_all | solution.py:17
  85.3 1.5 copy-done.1
  86.9 1.3 fusion.5
  88.1 0.5 broadcast_in_dim.10
  88.7 54.8 %all_to_all.16 = f32[4,512,512]{2,1,0:T(8,128)} all-to-all(f32[4,512,512]{2,1,0:T(8,128)S(1)} %broadcast_in_dim.10), channel_id=1, replica_groups=mesh['layer'=4,'latent_0'=4,'latent_1'=4,'latent_2'=4] {'layer'}, dimensions={0} | all-to-all | bytes 8388608 | tf_op jit(solution)/shard_map/all_to_all | solution.py:33
  143.4 2.8 reduce_sum.36
  146.2 0.7 fusion.11
  147.0 0.8 copy-done.5
  147.8 1.2 convolution_bitcast_fusion
  149.0 2.2 copy.21
  151.3 44.4 %reduce-scatter.4.cloned.1.call-done = f32[16,8,2048]{2,1,0:T(8,128)} async-done(((f32[64,8,2048]{2,1,0:T(8,128)}), f32[16,8,2048]{2,1,0:T(8,128)}) %reduce-scatter.4.cloned.1.call-update) | async-done | bytes 1048592 | tf_op jit(solution)/shard_map/reduce_scatter | solution.py:46
  195.7 9.8 %copy.22 = f32[16,8,2048]{1,2,0:T(8,128)} copy(f32[16,8,2048]{2,1,0:T(8,128)} %reduce-scatter.4.cloned.1.call-done) | data formatting | bytes 2097152 | tf_op jit(solution)/shard_map/reduce_scatter | solution.py:46
  205.5 150.4 %reduce-scatter.6.cloned.1.call-done = f32[4,8,2048]{1,2,0:T(8,128)} async-done(((f32[16,8,2048]{1,2,0:T(8,128)}), f32[4,8,2048]{1,2,0:T(8,128)}) %reduce-scatter.6.cloned.1.call-update) | async-done | bytes 262160 | tf_op jit(solution)/shard_map/reduce_scatter | solution.py:46
  356.0 3.0 split.8
  359.0 1.3 convert_reduce_fusion.2
  360.3 82.5 %reduce-scatter.8.cloned.1.call-done = f32[1,8,2048]{1,2,0:T(8,128)} async-done(((f32[4,8,2048]{1,2,0:T(8,128)}), f32[1,8,2048]{1,2,0:T(8,128)}) %reduce-scatter.8.cloned.1.call-update) | async-done | bytes 65552 | tf_op jit(solution)/shard_map/reduce_scatter | solution.py:46
  442.8 2.6 bitcast_subtract_fusion
  445.4 1.8 copy.23
  447.3 75.3 %all-gather.2.cloned.1.call-done = bf16[512,2048]{1,0:T(8,128)(2,1)} async-done(((bf16[8,2048]{1,0:T(8,128)(2,1)}), bf16[512,2048]{1,0:T(8,128)(2,1)}) %all-gather.2.cloned.1.call-update) | async-done | bytes 2097168 | tf_op jit(solution)/shard_map/all_gather | solution.py:85
  522.5 2.9 fusion.7
  525.4 1.5 broadcast_in_dim.11
  526.9 6.7 %all-to-all-start.2 = ((bf16[4,512,512]{2,1,0:T(8,128)(2,1)}), bf16[4,512,512]{2,1,0:T(8,128)(2,1)}, u32[]{:S(2)}, u32[]{:S(2)}) async-start(bf16[4,512,512]{2,1,0:T(8,128)(2,1)} %broadcast_in_dim.11), calls=%async_computation.5 | async-start | bytes 4194304 | tf_op jit(solution)/shard_map/all_to_all | solution.py:33
  533.7 2.1 convert_reduce_fusion
  535.8 0.6 fusion.13
  536.4 3.7 fusion.1
  540.0 18.6 %all-to-all-done.2 = bf16[4,512,512]{2,1,0:T(8,128)(2,1)} async-done(((bf16[4,512,512]{2,1,0:T(8,128)(2,1)}), bf16[4,512,512]{2,1,0:T(8,128)(2,1)}, u32[]{:S(2)}, u32[]{:S(2)}) %all-to-all-start.2) | async-done | bytes 2097184 | tf_op jit(solution)/shard_map/all_to_all | solution.py:33
  558.6 2.0 convert_reduce_fusion.1
  560.6 0.9 fusion.16
  561.5 0.8 copy-done.2
  562.4 2.6 fusion
  (20 shorter events, 0.5 us)
Async XLA Ops:
  7.2 140.6 %copy-start = (bf16[1,512,2048]{2,1,0:T(8,128)(2,1)S(1)}, bf16[1,512,2048]{2,1,0:T(8,128)(2,1)}, u32[]{:S(2)}) copy-start(bf16[1,512,2048]{2,1,0:T(8,128)(2,1)} %param.8) | copy-start | bytes 6291460
  7.2 188.5 %reduce-scatter.4.cloned.1.call-start = ((), (), s32[]{:S(2)}) async-start(), calls=%async_computation.6 | async-start | bytes 5242880 | tf_op jit(solution)/shard_map/reduce_scatter | solution.py:46
  9.1 77.8 %copy-start.3 = (bf16[1,2048,512]{2,1,0:T(8,128)(2,1)S(1)}, bf16[1,2048,512]{2,1,0:T(8,128)(2,1)}, u32[]{:S(2)}) copy-start(bf16[1,2048,512]{2,1,0:T(8,128)(2,1)} %param.6) | copy-start | bytes 6291460
  85.3 1.5 copy-start.1
  143.4 2.8 copy-start.6
  147.0 0.8 copy-start.5
  151.3 204.7 %reduce-scatter.6.cloned.1.call-start = ((), (), s32[]{:S(2)}) async-start(), calls=%async_computation.7 | async-start | bytes 20971520 | tf_op jit(solution)/shard_map/reduce_scatter | solution.py:46
  205.5 237.3 %reduce-scatter.8.cloned.1.call-start = ((), (), s32[]{:S(2)}) async-start(), calls=%async_computation.8 | async-start | bytes 5242880 | tf_op jit(solution)/shard_map/reduce_scatter | solution.py:46
  355.9 166.6 %all-gather.2.cloned.1.call-start = ((), (), s32[]{:S(2)}) async-start(), calls=%async_computation.9 | async-start | bytes 2129920 | tf_op jit(solution)/shard_map/all_gather | solution.py:85
  526.9 31.7 %all-to-all-start.2 = ((bf16[4,512,512]{2,1,0:T(8,128)(2,1)}), bf16[4,512,512]{2,1,0:T(8,128)(2,1)}, u32[]{:S(2)}, u32[]{:S(2)}) async-start(bf16[4,512,512]{2,1,0:T(8,128)(2,1)} %broadcast_in_dim.11), calls=%async_computation.5 | async-start | bytes 4194304 | tf_op jit(solution)/shard_map/all_to_all | solution.py:33
  533.7 2.7 copy-start.4
  560.6 1.7 copy-start.2
Sparse Core Ops, SparseCore 0:
  151.4 44.2 reduce-scatter.3
  205.6 150.2 reduce-scatter.5
  358.5 84.2 reduce-scatter.7
  447.4 75.1 all-gather.1
